TPU v7x, 128 devices: a whole 4x4x4 slice. The times are simulated.
128 devices in a mesh: row: 8 (over y_lo, z), col: 16 (over x, y_hi, core).
Axes of the slice: x: 4, y: 4 (y_hi: 2, y_lo: 2; y = y_hi * 2 + y_lo), z: 4, core: 2. Of those that a mesh axis runs over, the one named last changes fastest.
Arguments:
- layer_input: bfloat16 [8192, 7168], P('row', 'col'), may hold values from -6 to 6
- output_grad: bfloat16 [8192, 7168], P('row', 'col'), may hold values from -6 to 6
- gate_pre: bfloat16 [8192, 4864], P('row', 'col'), may hold values from -8 to 8
- up_pre: bfloat16 [8192, 4864], P('row', 'col'), may hold values from -6 to 6
- down_weight: bfloat16 [4864, 7168], P('col', 'row'), may hold values from -0.078125 to 0.078125
- route_ids: int32 [8192, 2], P('row'), may hold values from 0 to 127, all different within a row; in each aligned block of 1024 rows (0 to 1023, 1024 to 2047, ...) at most 24 rows name the same one
- route_gates: float32 [8192, 2], P('row'), may hold values from 0.2 to 1
- expert_gate: bfloat16 [8, 7168, 2432], P('row', None, 'col'), may hold values from -0.0625 to 0.0625
- expert_up: bfloat16 [8, 7168, 2432], P('row', None, 'col'), may hold values from -0.0625 to 0.0625
- expert_down: bfloat16 [8, 2432, 7168], P('row', 'col'), may hold values from -0.078125 to 0.078125
Outputs:
- gate_pre_grad: bfloat16 [8192, 4864], P('row', 'col')
- up_pre_grad: bfloat16 [8192, 4864], P('row', 'col')
- down_weight_grad: bfloat16 [4864, 7168], P('col', 'row')
- expert_gate_grad: bfloat16 [8, 7168, 2432], P('row', None, 'col')
- expert_up_grad: bfloat16 [8, 7168, 2432], P('row', None, 'col')
- expert_down_grad: bfloat16 [8, 2432, 7168], P('row', 'col')
- moe_input_grad: bfloat16 [8192, 7168], P('row', 'col')
Inputs may be any that keep to these rules, and one draw needn't show every extreme that they name: `route_ids`: each row names two different experts. Among the 1024 rows of one index of row, no expert is named by more than 24 rows, a bound that some block reaches.
All inputs are finite; a program needn't handle non-finite values.
Results may differ from a plain program's by a relative error of at most 0.02.
Values may be sent and summed in bfloat16 or wider, within the bound.
A program may use at most 192 MiB of HBM per device.

v0:
```python
import jax
import jax.numpy as jnp
from jax import lax
from jax.sharding import PartitionSpec as P

CAP = 24


def silu_slope(values):
    sigma = jax.nn.sigmoid(values)
    return sigma * (1.0 + values * (1.0 - sigma))


def slot_tables(route_block, gate_block, windows, capacity):
    count = route_block.shape[0]
    routes = route_block.reshape(-1)
    experts = jnp.arange(windows, dtype=jnp.int32)
    hits = (routes[:, None] == experts[None, :]).astype(jnp.int32)
    ranks = jnp.cumsum(hits, axis=0) - hits
    places = jnp.arange(capacity, dtype=jnp.int32)
    matched = hits[:, :, None] * (ranks[:, :, None] == places[None, None, :]).astype(jnp.int32)
    matched = matched.reshape(count, 2, windows, capacity).astype(jnp.float32)
    picked = jnp.sum(matched, axis=1)
    weighed = jnp.einsum("tkec,tk->ec", matched, gate_block, precision=lax.Precision.HIGHEST)
    return (picked, weighed)


def body(
    layer_input,
    output_grad,
    gate_pre,
    up_pre,
    down_weight,
    route_ids,
    route_gates,
    expert_gate,
    expert_up,
    expert_down,
):
    row_count = lax.axis_size("row")
    windows = row_count // 2
    panel = lax.all_gather(output_grad, "col", axis=1, tiled=True)
    columns = panel
    hidden_grad = lax.dot_general(
        columns,
        lax.all_gather(down_weight, "row", axis=1, tiled=True),
        (((1,), (1,)), ((), ())),
        preferred_element_type=jnp.float32,
    )
    gate_float = gate_pre.astype(jnp.float32)
    up_float = up_pre.astype(jnp.float32)
    activated = jax.nn.silu(gate_float)
    hidden = (activated * up_float).astype(jnp.bfloat16)
    up_pre_grad = (hidden_grad * activated).astype(jnp.bfloat16)
    gate_pre_grad = (hidden_grad * up_float * silu_slope(gate_float)).astype(jnp.bfloat16)
    columns = panel
    summed = lax.psum_scatter(
        lax.dot_general(
            columns, hidden, (((0,), (0,)), ((), ())), preferred_element_type=jnp.float32
        ).astype(jnp.bfloat16),
        "row",
        scatter_dimension=0,
        tiled=True,
    ).astype(jnp.float32)
    down_weight_grad = summed.T.astype(jnp.bfloat16)
    picked, weighed = slot_tables(route_ids, route_gates, windows, CAP)
    picked_half = picked.astype(jnp.bfloat16)
    chosen_rows = jnp.einsum(
        "tec,td->ecd", picked_half, layer_input, preferred_element_type=jnp.float32
    ).astype(jnp.bfloat16)
    chosen_out = jnp.einsum(
        "tec,td->ecd", picked_half, output_grad, preferred_element_type=jnp.float32
    )
    chosen_cots = (chosen_out * weighed[:, :, None]).astype(jnp.bfloat16)
    wide_rows, wide_cots = (
        lax.all_gather(chosen_rows, "col", axis=2, tiled=True),
        lax.all_gather(chosen_cots, "col", axis=2, tiled=True),
    )
    recv_rows, recv_cots = (
        lax.all_to_all(
            jnp.repeat(wide_rows, 2, axis=0), "row", split_axis=0, concat_axis=0, tiled=True
        ),
        lax.all_to_all(
            jnp.repeat(wide_cots, 2, axis=0), "row", split_axis=0, concat_axis=0, tiled=True
        ),
    )
    width = recv_rows.shape[2]
    rows_x = recv_rows.reshape(-1, width)
    rows_d = recv_cots.reshape(-1, width)
    weight_gate = expert_gate[0]
    weight_up = expert_up[0]
    weight_down = expert_down[0]
    gate_value = jnp.dot(rows_x, weight_gate, preferred_element_type=jnp.float32)
    up_value = jnp.dot(rows_x, weight_up, preferred_element_type=jnp.float32)
    active = jax.nn.silu(gate_value)
    inner = (active * up_value).astype(jnp.bfloat16)
    inner_grad = lax.dot_general(
        rows_d, weight_down, (((1,), (1,)), ((), ())), preferred_element_type=jnp.float32
    )
    down_local = lax.dot_general(
        inner, rows_d, (((0,), (0,)), ((), ())), preferred_element_type=jnp.float32
    ).astype(jnp.bfloat16)
    up_local = (inner_grad * active).astype(jnp.bfloat16)
    gate_local = (inner_grad * up_value * silu_slope(gate_value)).astype(jnp.bfloat16)
    gate_grad = lax.dot_general(
        rows_x, gate_local, (((0,), (0,)), ((), ())), preferred_element_type=jnp.float32
    ).astype(jnp.bfloat16)
    up_grad = lax.dot_general(
        rows_x, up_local, (((0,), (0,)), ((), ())), preferred_element_type=jnp.float32
    ).astype(jnp.bfloat16)
    partial_value = lax.dot_general(
        gate_local, weight_gate, (((1,), (1,)), ((), ())), preferred_element_type=jnp.float32
    )
    partial_value = partial_value + lax.dot_general(
        up_local, weight_up, (((1,), (1,)), ((), ())), preferred_element_type=jnp.float32
    )
    partial_value = partial_value.reshape(row_count, CAP, width)
    reduced = lax.psum_scatter(
        partial_value.astype(jnp.bfloat16), "col", scatter_dimension=2, tiled=True
    ).astype(jnp.float32)
    arrived = lax.all_to_all(
        reduced.astype(jnp.bfloat16), "row", split_axis=0, concat_axis=0, tiled=True
    ).astype(reduced.dtype)
    combined = jnp.sum(arrived.reshape(windows, 2, CAP, arrived.shape[2]), axis=1)
    moe_input_grad = jnp.einsum(
        "tec,ecd->td", picked, combined, precision=lax.Precision.HIGHEST
    ).astype(jnp.bfloat16)
    return (
        gate_pre_grad,
        up_pre_grad,
        down_weight_grad,
        gate_grad[None],
        up_grad[None],
        down_local[None],
        moe_input_grad,
    )


def solution(mesh):
    in_specs = (
        P("row", "col"),
        P("row", "col"),
        P("row", "col"),
        P("row", "col"),
        P("col", "row"),
        P("row", None),
        P("row", None),
        P("row", None, "col"),
        P("row", None, "col"),
        P("row", "col", None),
    )
    out_specs = (
        P("row", "col"),
        P("row", "col"),
        P("col", "row"),
        P("row", None, "col"),
        P("row", None, "col"),
        P("row", "col", None),
        P("row", "col"),
    )
    return jax.shard_map(body, mesh=mesh, in_specs=in_specs, out_specs=out_specs, check_vma=False)
```

profile of v0, /device:TPU:99, one launch (start us, length us, event | category | flops | bytes accessed | tf_op | source)
XLA Modules:
  0.0 489.5 jit_solution(9682354927380486234)
XLA Ops:
  7.2 0.9 fusion.36
  8.1 0.9 copy.31
  9.0 0.3 eq.55
  9.3 0.3 eq.51
  9.5 1.2 reduce-window.6
  11.2 0.4 copy.41
  11.6 1.3 bitcast_subtract_fusion
  12.9 1.5 copy.34
  14.5 2.2 convolution_convert_fusion.4
  16.8 1.9 copy.35
  18.7 2.7 fusion.25
  21.5 1.1 fusion.22
  22.6 1.9 copy.37
  24.6 0.7 all-gather.5.cloned.1.call-update
  25.2 62.6 %all-gather.9.cloned.1.call-done = bf16[4,24,7168]{1,0,2:T(4,128)(2,1)} async-done(((bf16[4,24,448]{1,0,2:T(4,128)(2,1)}), bf16[4,24,7168]{1,0,2:T(4,128)(2,1)}) %all-gather.9.cloned.1.call-update) | async-done | bytes 1376272 | tf_op jit(solution)/shard_map/all_gather | solution.py:76
  87.8 9.7 %copy.36 = bf16[4,24,7168]{2,1,0:T(8,128)(2,1)} copy(bf16[4,24,7168]{1,0,2:T(4,128)(2,1)} %all-gather.9.cloned.1.call-done) | data formatting | bytes 2752512 | tf_op jit(solution)/shard_map/all_gather | solution.py:76
  97.6 3.1 broadcast_in_dim.20
  100.7 4.4 all-to-all-start
  105.1 64.3 %all-gather.11.cloned.1.call-done = bf16[4,24,7168]{1,0,2:T(4,128)(2,1)} async-done(((bf16[4,24,448]{1,0,2:T(4,128)(2,1)}), bf16[4,24,7168]{1,0,2:T(4,128)(2,1)}) %all-gather.11.cloned.1.call-update) | async-done | bytes 1376272 | tf_op jit(solution)/shard_map/all_gather | solution.py:77
  169.4 9.7 %copy.38 = bf16[4,24,7168]{2,1,0:T(8,128)(2,1)} copy(bf16[4,24,7168]{1,0,2:T(4,128)(2,1)} %all-gather.11.cloned.1.call-done) | data formatting | bytes 2752512 | tf_op jit(solution)/shard_map/all_gather | solution.py:77
  179.1 3.2 broadcast_in_dim.21
  182.3 4.3 all-to-all-start.1
  186.7 2.9 fusion.7
  189.7 2.8 fusion.10
  192.5 37.2 %all-to-all-done.1 = bf16[8,24,7168]{2,1,0:T(8,128)(2,1)} async-done(((bf16[8,24,7168]{2,1,0:T(8,128)(2,1)}), bf16[8,24,7168]{2,1,0:T(8,128)(2,1)}, u32[]{:S(2)}, u32[]{:S(2)}) %all-to-all-start.1) | async-done | bytes 2752544 | tf_op jit(solution)/shard_map/all_to_all | solution.py:83
  229.7 3.5 multiply_convert_fusion.2
  233.2 0.9 fusion.5
  234.1 0.7 copy-done.3
  234.8 2.5 fusion.1
  237.3 13.5 %copy.44 = bf16[8,24,7168]{1,0,2:T(8,128)(2,1)} copy(bf16[8,24,7168]{2,1,0:T(8,128)(2,1)} %bitcast.71) | data formatting | bytes 5505024
  250.8 17.9 %reshape.96 = bf16[7168,192]{1,0:T(8,128)(2,1)} reshape(bf16[7168,8,24]{2,1,0:T(8,128)(2,1)} %bitcast.68) | data formatting | bytes 5505024
  268.8 0.5 all-gather.7.cloned.1.call-update
  269.3 0.2 reduce-scatter.7.cloned.1.call-start
  269.6 12.4 %all-gather.5.cloned.1.call-done = bf16[1024,7168]{0,1:T(8,128)(2,1)} async-done(((bf16[1024,448]{0,1:T(8,128)(2,1)}), bf16[1024,7168]{0,1:T(8,128)(2,1)}) %all-gather.5.cloned.1.call-update) | async-done | bytes 14680080 | tf_op jit(solution)/shard_map/all_gather | solution.py:42
  282.0 16.3 %fusion = bf16[7168,304]{0,1:T(8,128)(2,1)} fusion(bf16[1024,7168]{0,1:T(8,128)(2,1)} %all-gather.5.cloned.1.call-done, bf16[1024,304]{0,1:T(8,128)(2,1)S(1)} %copy-done.6, bf16[1024,304]{0,1:T(8,128)(2,1)S(1)} %copy-done.5), kind=kOutput, calls=%fused_computation.2 | convolution fusion | flops 4467408896 | bytes 20283392 | tf_op jit(solution)/shard_map/dot_general | solution.py:58
  298.3 7.7 %copy.42 = bf16[7168,304]{1,0:T(8,128)(2,1)} copy(bf16[7168,304]{0,1:T(8,128)(2,1)} %fusion) | data formatting | bytes 8716288
  306.0 3.9 fusion.3
  309.9 3.9 fusion.4
  313.8 46.3 %reduce-scatter.9.cloned.1.call-done = bf16[448,192]{1,0:T(8,128)(2,1)} async-done(((bf16[7168,192]{1,0:T(8,128)(2,1)}), bf16[448,192]{1,0:T(8,128)(2,1)}) %reduce-scatter.9.cloned.1.call-update) | async-done | bytes 172048
  360.1 1.7 reshape.97
  361.8 1.3 copy.45
  363.2 4.2 all-to-all-start.2
  367.4 3.9 fusion.2
  371.2 2.6 bitcast_convert_fusion
  373.8 41.1 %all-gather.7.cloned.1.call-done = bf16[304,7168]{1,0:T(8,128)(2,1)} async-done(((bf16[304,896]{1,0:T(8,128)(2,1)}), bf16[304,7168]{1,0:T(8,128)(2,1)}) %all-gather.7.cloned.1.call-update) | async-done | bytes 4358160 | tf_op jit(solution)/shard_map/all_gather | solution.py:46
  414.9 12.9 %multiply_convert_fusion = (bf16[1024,304]{0,1:T(8,128)(2,1)}, bf16[1024,304]{0,1:T(8,128)(2,1)}) fusion(bf16[1024,304]{0,1:T(8,128)(2,1)} %param.12, bf16[1024,304]{0,1:T(8,128)(2,1)} %param.13, bf16[304,7168]{1,0:T(8,128)(2,1)} %all-gather.7.cloned.1.call-done, bf16[1024,7168]{0,1:T(8,128)(2,1)} %all-gather.5.cloned.1.call-done), kind=kOutput, calls=%fused_computation.33 | convolution fusion | flops 4467408896 | bytes 21528576 | tf_op jit(solution)/shard_map/dot_general | solution.py:44
  427.7 52.8 %reduce-scatter.7.cloned.1.call-done = bf16[896,304]{1,0:T(8,128)(2,1)} async-done(((bf16[7168,304]{1,0:T(8,128)(2,1)}), bf16[896,304]{1,0:T(8,128)(2,1)}) %reduce-scatter.7.cloned.1.call-update) | async-done | bytes 544784
  480.5 2.1 copy.43
  (30 shorter events, 0.9 us)
Async XLA Ops:
  7.2 179.5 %copy-start = (bf16[1,7168,152]{1,2,0:T(8,128)(2,1)S(1)}, bf16[1,7168,152]{1,2,0:T(8,128)(2,1)}, u32[]{:S(2)}) copy-start(bf16[1,7168,152]{1,2,0:T(8,128)(2,1)} %param.17) | copy-start | bytes 6537220
  7.2 80.7 %all-gather.9.cloned.1.call-start = ((), (), s32[]{:S(2)}) async-start(), calls=%async_computation.7 | async-start | bytes 7798784 | tf_op jit(solution)/shard_map/all_gather | solution.py:76
  12.9 8.6 %copy-start.4 = (bf16[1024,448]{0,1:T(8,128)(2,1)S(1)}, bf16[1024,448]{0,1:T(8,128)(2,1)}, u32[]{:S(2)}) copy-start(bf16[1024,448]{0,1:T(8,128)(2,1)} %param.11) | copy-start | bytes 2752516
  18.7 150.7 %all-gather.11.cloned.1.call-start = ((), (), s32[]{:S(2)}) async-start(), calls=%async_computation.8 | async-start | bytes 7798784 | tf_op jit(solution)/shard_map/all_gather | solution.py:77
  24.5 257.5 %all-gather.5.cloned.1.call-start = ((), (), s32[]{:S(2)}) async-start(), calls=%async_computation.5 | async-start | bytes 15597568 | tf_op jit(solution)/shard_map/all_gather | solution.py:42
  100.7 78.4 %all-to-all-start = ((bf16[8,24,7168]{2,1,0:T(8,128)(2,1)}), bf16[8,24,7168]{2,1,0:T(8,128)(2,1)}, u32[]{:S(2)}, u32[]{:S(2)}) async-start(bf16[8,24,7168]{2,1,0:T(8,128)(2,1)} %bitcast.69), calls=%async_computation | async-start | bytes 5505024 | tf_op jit(solution)/shard_map/all_to_all | solution.py:80
  182.3 47.4 %all-to-all-start.1 = ((bf16[8,24,7168]{2,1,0:T(8,128)(2,1)}), bf16[8,24,7168]{2,1,0:T(8,128)(2,1)}, u32[]{:S(2)}, u32[]{:S(2)}) async-start(bf16[8,24,7168]{2,1,0:T(8,128)(2,1)} %bitcast.70), calls=%async_computation.1 | async-start | bytes 5505024 | tf_op jit(solution)/shard_map/all_to_all | solution.py:83
  186.7 173.4 %reduce-scatter.9.cloned.1.call-start = ((), (), s32[]{:S(2)}) async-start(), calls=%async_computation.10 | async-start | bytes 3899392
  186.7 3.0 copy-start.2
  233.2 1.6 copy-start.3
  268.7 13.3 %copy-start.5 = (bf16[1024,304]{0,1:T(8,128)(2,1)S(1)}, bf16[1024,304]{0,1:T(8,128)(2,1)}, u32[]{:S(2)}) copy-start(bf16[1024,304]{0,1:T(8,128)(2,1)} %param.12) | copy-start | bytes 1867780
  268.7 13.3 %copy-start.6 = (bf16[1024,304]{0,1:T(8,128)(2,1)S(1)}, bf16[1024,304]{0,1:T(8,128)(2,1)}, u32[]{:S(2)}) copy-start(bf16[1024,304]{0,1:T(8,128)(2,1)} %param.13) | copy-start | bytes 1867780
  268.7 146.1 %all-gather.7.cloned.1.call-start = ((), (), s32[]{:S(2)}) async-start(), calls=%async_computation.6 | async-start | bytes 4902912 | tf_op jit(solution)/shard_map/all_gather | solution.py:46
  269.3 211.2 %reduce-scatter.7.cloned.1.call-start = ((), (), s32[]{:S(2)}) async-start(), calls=%async_computation.9 | async-start | bytes 6193152
  363.2 8.1 %all-to-all-start.2 = ((bf16[8,24,448]{2,1,0:T(8,128)(2,1)}), bf16[8,24,448]{2,1,0:T(8,128)(2,1)S(1)}, u32[]{:S(2)}, u32[]{:S(2)}) async-start(bf16[8,24,448]{2,1,0:T(8,128)(2,1)} %copy.45), calls=%async_computation.2 | async-start | bytes 393216 | tf_op jit(solution)/shard_map/all_to_all | solution.py:121
  414.9 67.8 %copy-start.1 = (bf16[1,7168,152]{1,2,0:T(8,128)(2,1)S(1)}, bf16[1,7168,152]{1,2,0:T(8,128)(2,1)}, u32[]{:S(2)}) copy-start(bf16[1,7168,152]{1,2,0:T(8,128)(2,1)} %param.17) | copy-start | bytes 6537220
Sparse Core Ops, SparseCore 0:
  18.8 68.9 all-gather.8
  90.8 78.5 all-gather.10
  171.8 110.0 all-gather.4
  285.9 74.1 reduce-scatter.8
  361.6 53.2 all-gather.6
  417.2 63.2 reduce-scatter.6
where the time goes:
time: 496 us; the launch traced here: 489 us
  waiting for transfers between devices  318 us (64%)
  local copies, waits for them, and re-layouts  78.2 us (16%)
  matrix products  62.1 us (13%)
  between operations  14.3 us (3%)
  starting transfers between devices  13.4 us (3%)
    unnamed x8, waiting for transfers between devices  100 us
    all_gather x1, waiting for transfers between devices, body(): lax.all_gather(chosen_cots, 'col', axis=2, tiled=True)  64.3 us
    all_gather x1, waiting for transfers between devices, body(): lax.all_gather(chosen_rows, 'col', axis=2, tiled=True)  62.6 us
    unnamed x21, local copies, waits for them, and re-layouts  46 us
    all_gather x1, waiting for transfers between devices, body(): lax.all_gather(down_weight, 'row', axis=1, tiled=True)  41.1 us
    all_to_all x1, waiting for transfers between devices, body(): lax.all_to_all(jnp.repeat(wide_cots, 2, axis=0), 'row', split_axis=0, con...  37.2 us
    dot_general x1, matrix products, body(): lax.dot_general(columns, hidden, (((0,), (0,)), ((), ())), preferred_elem...  16.3 us
    dot_general x1, matrix products, body(): lax.dot_general(columns, lax.all_gather(down_weight, 'row', axis=1, tiled...  12.9 us
  transfers between devices with their start and end apart: 9, of which 7 were waited for; matrix products, arithmetic and copies ran while one was open for 26% of the time, Pallas kernels for 0%

commit v1 on v0

v1 whole, which is shorter than its diff:
```python
import jax
import jax.numpy as jnp
from jax import lax
from jax.experimental import pallas as pl
from jax.experimental.pallas import tpu as pltpu
from jax.sharding import PartitionSpec as P

TOK = 1024
FEAT = 448
PAIR = 2 * FEAT
FFD = 304
HID = 152
ROWS = 8
CHIPS = 8
WIN = 4
CAP = 24
PAD = 32
SLOTS = ROWS * CAP
HALF = SLOTS // 2

F32 = jnp.float32
BF16 = jnp.bfloat16
MESH = pl.DeviceIdType.MESH

NN = (((1,), (0,)), ((), ()))
NT = (((1,), (1,)), ((), ()))
TN = (((0,), (0,)), ((), ()))


def dot(a, b, dims):
    return lax.dot_general(a, b, dims, preferred_element_type=F32)


def slope_of(values, sigma):
    return sigma * (1.0 + values * (1.0 - sigma))


class Channels:
    def __init__(self, send, recv):
        self.send, self.recv, self.used, self.sent = send, recv, 0, []

    def take(self, count=1):
        first = self.used
        self.used += count
        return first

    def copy(self, src, dst, device, index=None):
        index = self.take() if index is None else index
        return pltpu.make_async_remote_copy(
            src_ref=src,
            dst_ref=dst,
            send_sem=self.send.at[index],
            recv_sem=self.recv.at[index],
            device_id=device,
            device_id_type=MESH,
        )

    def go(self, src, dst, device):
        made = self.copy(src, dst, device)
        made.start()
        self.sent.append(made)
        return made


CHANNELS = 128


class RingPair:
    def __init__(self, ch, slot, cut, size, pos, side, right, left, across):
        self.ch, self.slot, self.cut, self.size = ch, slot, cut, size
        self.pos, self.side = pos, side
        self.right, self.left, self.across = right, left, across

    def at(self, delta, flip):
        return self.slot((self.pos + delta) % 4, (self.side + flip) % 2)

    def own(self, src):
        dst = self.at(0, 0)
        self.a = self.ch.go(src, dst, self.right)
        self.b = self.ch.go(src, dst, self.left)
        self.c = self.ch.go(src, dst, self.across)

    def wait_own(self):
        self.a.wait_recv()
        self.b.wait_recv()
        self.c.wait_recv()

    def _far(self, flip):
        lo, hi = pl.ds(0, self.cut), pl.ds(self.cut, self.size - self.cut)
        from_left, from_right = self.at(3, flip), self.at(1, flip)
        return (
            self.ch.go(from_left.at[lo], from_left.at[lo], self.right),
            self.ch.go(from_right.at[hi], from_right.at[hi], self.left),
        )

    def far(self):
        self.d = self._far(0)

    def wait_far(self):
        self.d[0].wait_recv()
        self.d[1].wait_recv()

    def other(self):
        src = self.at(0, 1)
        self.e = (self.ch.go(src, src, self.right), self.ch.go(src, src, self.left))

    def wait_other(self):
        self.e[0].wait_recv()
        self.e[1].wait_recv()

    def other_far(self):
        self.f = self._far(1)

    def wait_other_far(self):
        self.f[0].wait_recv()
        self.f[1].wait_recv()


def kernel(
    ids_ref, gates_ref, gp_ref, up_ref, og, li, dw, wg, wu, wd,
    gpg_ref, upg_ref, dwg_ref, gg, ug, dg, mig_ref,
    panel, li_pair, dw_all, d_send, d_recv, rows, w_gate, w_up, w_down,
    e_part, e_sib, e_sum, e_recv, c_send, c_recv, g_send, f_recv,
    picked, hidden, hg, mids, back, send_sems, recv_sems, local_sems,
):
    r = lax.axis_index("row")
    c = lax.axis_index("col")
    yl, z = r // 4, r % 4
    x, yh, k = c // 4, (c // 2) % 2, c % 2
    chip = c // 2

    def row_of(yl_, z_):
        return yl_ * 4 + z_

    def chip_of(x_, yh_):
        return x_ * 2 + yh_

    def col_dev(x_, yh_):
        return (r, chip_of(x_, yh_) * 2 + k)

    def row_dev(row_):
        return (row_, c)

    sib = (r, chip * 2 + (1 - k))

    barrier = pltpu.get_barrier_semaphore()
    greeted = 0
    for o in range(1, 8):
        pl.semaphore_signal(barrier, inc=1, device_id=row_dev((r + o) % 8), device_id_type=MESH)
        pl.semaphore_signal(
            barrier, inc=1, device_id=col_dev((x + o // 2) % 4, (yh + o % 2) % 2), device_id_type=MESH
        )
        greeted += 2
    for o in range(8):
        pl.semaphore_signal(
            barrier, inc=1, device_id=((r + o) % 8, chip * 2 + (1 - k)), device_id_type=MESH
        )
        greeted += 1
    pl.semaphore_wait(barrier, greeted)

    ch = Channels(send_sems, recv_sems)
    lanes = pl.ds(pl.multiple_of(k * FEAT, FEAT), FEAT)

    def panel_slot(x_, yh_):
        return panel.at[chip_of(x_, yh_), lanes]

    def rows_slot(x_, yh_):
        return rows.at[k, chip_of(x_, yh_)]

    def dw_slot(z_, yl_):
        return dw_all.at[row_of(yl_, z_)]

    x_right, x_left, y_across = col_dev((x + 1) % 4, yh), col_dev((x + 3) % 4, yh), col_dev(x, 1 - yh)
    ga = RingPair(ch, panel_slot, FEAT // 2, FEAT, x, yh, x_right, x_left, y_across)
    gc = RingPair(ch, rows_slot, HALF, SLOTS, x, yh, x_right, x_left, y_across)
    gb = RingPair(
        ch, dw_slot, 160, FFD, z, yl,
        row_dev(row_of(yl, (z + 1) % 4)), row_dev(row_of(yl, (z + 3) % 4)), row_dev(row_of(1 - yl, z)),
    )

    li_slot = li_pair.at[lanes]
    own_slot = panel_slot(x, yh)
    sib_og = ch.go(og, own_slot, sib)
    sib_li = ch.go(li, li_slot, sib)
    ga.own(og)
    gb.own(dw)
    local = [
        pltpu.make_async_copy(og, own_slot, local_sems.at[0]),
        pltpu.make_async_copy(li, li_slot, local_sems.at[1]),
        pltpu.make_async_copy(dw, dw_slot(z, yl), local_sems.at[2]),
        pltpu.make_async_copy(wg, w_gate, local_sems.at[3]),
        pltpu.make_async_copy(wu, w_up, local_sems.at[4]),
        pltpu.make_async_copy(wd, w_down, local_sems.at[5]),
    ]
    for each in local:
        each.start()

    ids0, ids1 = ids_ref[0:1, :], ids_ref[1:2, :]
    expert = lax.broadcasted_iota(jnp.int32, (8, TOK), 0)
    lane = lax.broadcasted_iota(jnp.int32, (8, TOK), 1)
    first = (jnp.broadcast_to(ids0, (8, TOK)) == expert).astype(F32)
    second = (jnp.broadcast_to(ids1, (8, TOK)) == expert).astype(F32)
    hits = first + second
    ranks = hits
    step = 1
    while step < TOK:
        ranks = ranks + jnp.where(lane >= step, pltpu.roll(ranks, step, 1), 0.0)
        step *= 2
    ranks = (ranks - hits).astype(jnp.int32)
    gate_of = first * gates_ref[0:1, :] + second * gates_ref[1:2, :]
    place = lax.broadcasted_iota(jnp.int32, (PAD, TOK), 0)
    weights = []
    for e in range(WIN):
        same = jnp.broadcast_to(ranks[e : e + 1, :], (PAD, TOK)) == place
        mine = jnp.where(same & (place < CAP), jnp.broadcast_to(hits[e : e + 1, :], (PAD, TOK)), 0.0)
        picked[pl.ds(e * PAD, PAD), :] = mine.astype(BF16)
        weights.append(jnp.sum(mine * gate_of[e : e + 1, :], axis=1, keepdims=True))
    weights = jnp.concatenate(weights, axis=0)

    local[0].wait()
    local[1].wait()
    sib_og.wait_recv()
    sib_li.wait_recv()

    @pl.when(k == 0)
    def _():
        chosen = dot(picked[...], li_pair[...], NT)
        c_send[...] = chosen.astype(BF16).reshape(WIN, PAD, PAIR)

    @pl.when(k == 1)
    def _():
        chosen = dot(picked[...], panel[chip], NT) * weights
        c_send[...] = chosen.astype(BF16).reshape(WIN, PAD, PAIR)

    to_experts = []
    for o in range(1, 8):
        dest = (r + o) % 8
        to_experts.append(ch.go(c_send.at[dest // 2], c_recv.at[r], row_dev(dest)))
    keep = pltpu.make_async_copy(c_send.at[r // 2], c_recv.at[r], local_sems.at[6])
    keep.start()

    def hide(i, carry):
        part = pl.ds(pl.multiple_of(i * 16, 16), 16)
        v = gp_ref[part, :].astype(F32)
        hidden[part, :] = (v * jax.nn.sigmoid(v) * up_ref[part, :].astype(F32)).astype(BF16)
        return carry

    lax.fori_loop(0, FFD // 16, hide, 0)

    for each in to_experts:
        each.wait_recv()
    keep.wait()
    packed = c_recv[...].astype(F32)[:, :CAP, :].reshape(SLOTS, PAIR).astype(BF16)
    rows[k, chip] = packed
    gc_own = gc.at(0, 0)
    c_sib = {(0, 0): ch.go(gc_own, gc_own, sib)}
    gc.own(gc_own)

    d_first = ch.take(8)

    def down_block(o):
        j = chip_of((x + o // 2) % 4, (yh + o % 2) % 2)
        d_send[j] = dot(hidden[...], panel[j], NT).astype(BF16)

        @pl.when(j != r)
        def _():
            down_copy(j).start()

    def down_copy(j):
        return pltpu.make_async_remote_copy(
            src_ref=d_send.at[j],
            dst_ref=d_recv.at[r],
            send_sem=send_sems.at[d_first + j],
            recv_sem=recv_sems.at[d_first + r],
            device_id=row_dev(j),
            device_id_type=MESH,
        )

    def forward(gather, kept, offsets):
        for o in offsets:
            slot = gather.at(o // 2, o % 2)
            kept[(o // 2, o % 2)] = ch.go(slot, slot, sib)

    down_block(0)

    a_sib = {}
    ga.wait_own()
    forward(ga, a_sib, (1, 2, 6))
    ga.far()
    gb.wait_own()
    gb.far()
    gb.other()

    gc.wait_own()
    gc.other()
    gc.far()
    forward(gc, c_sib, (1, 2, 6))

    for o in (1, 2, 6):
        a_sib[(o // 2, o % 2)].wait_recv()

    def near(i, carry):
        down_block(jnp.where(i == 0, 1, jnp.where(i == 1, 2, 6)))
        return carry

    lax.fori_loop(0, 3, near, 0)

    gc.wait_other()
    gc.other_far()
    gc.wait_far()
    forward(gc, c_sib, (3, 4, 7))
    ga.wait_far()
    forward(ga, a_sib, (4,))
    ga.other()
    gb.wait_other()
    gb.other_far()
    gb.wait_far()
    gc.wait_other_far()
    forward(gc, c_sib, (5,))
    a_sib[(2, 0)].wait_recv()
    down_block(4)
    for each in c_sib.values():
        each.wait_recv()
    for each in local[3:]:
        each.wait()

    mids[...] = jnp.zeros_like(mids)

    def lanes_of(i):
        return pl.ds(pl.multiple_of(i * PAIR, 128), PAIR)

    def enter(i, carry):
        part = lanes_of(i)
        taken = rows[0, i]
        mids[0] += dot(taken, w_gate[:, part], NT)
        mids[1] += dot(taken, w_up[:, part], NT)
        mids[2] += dot(rows[1, i], w_down[:, part], NT)
        return carry

    lax.fori_loop(0, CHIPS, enter, 0)
    gate_value, up_value, inner_grad = mids[0], mids[1], mids[2]
    sigma = jax.nn.sigmoid(gate_value)
    active = gate_value * sigma
    inner = (active * up_value).astype(BF16)
    up_local = (inner_grad * active).astype(BF16)
    gate_local = (inner_grad * up_value * slope_of(gate_value, sigma)).astype(BF16)

    def leave(i, carry):
        part = lanes_of(i)
        total = dot(gate_local, w_gate[:, part], NN) + dot(up_local, w_up[:, part], NN)
        e_part[i] = total.astype(BF16)
        return carry

    lax.fori_loop(0, CHIPS, leave, 0)

    mine = pl.ds(pl.multiple_of(k * HALF, HALF), HALF)
    theirs = pl.ds(pl.multiple_of((1 - k) * HALF, HALF), HALF)
    between = ch.go(e_part.at[:, theirs], e_sib, sib)

    ga.wait_other()
    ga.other_far()
    forward(ga, a_sib, (3, 7))
    between.wait_recv()

    def add_sib(i, carry):
        e_sum[i] = (e_part[i, mine].astype(F32) + e_sib[i].astype(F32)).astype(BF16)
        return carry

    lax.fori_loop(0, CHIPS, add_sib, 0)
    to_chips = []
    for o in range(1, 8):
        x_, yh_ = (x + o // 2) % 4, (yh + o % 2) % 2
        to_chips.append(ch.go(e_sum.at[chip_of(x_, yh_)], e_recv.at[o], col_dev(x_, yh_)))

    def grads(i, carry):
        part = lanes_of(i)
        taken = rows[0, i]
        w_gate[:, part] = dot(gate_local, taken, TN).astype(BF16)
        w_up[:, part] = dot(up_local, taken, TN).astype(BF16)
        w_down[:, part] = dot(inner, rows[1, i], TN).astype(BF16)
        return carry

    lax.fori_loop(0, CHIPS, grads, 0)
    stores = [
        pltpu.make_async_copy(w_gate, gg, local_sems.at[7]),
        pltpu.make_async_copy(w_up, ug, local_sems.at[8]),
        pltpu.make_async_copy(w_down, dg, local_sems.at[9]),
    ]
    for each in stores:
        each.start()

    a_sib[(1, 1)].wait_recv()
    a_sib[(3, 1)].wait_recv()

    def partner(i, carry):
        down_block(jnp.where(i == 0, 3, 7))
        return carry

    lax.fori_loop(0, 2, partner, 0)

    gb.wait_other_far()
    local[2].wait()

    def hidden_block(o):
        j = chip_of((x + o // 2) % 4, (yh + o % 2) % 2)
        return dot(dw_all[j], panel[j], NN)

    hg[...] = hidden_block(0)

    def accumulate(i, carry):
        hg[...] += hidden_block(jnp.where(i < 5, i, i + 1))
        return carry

    lax.fori_loop(1, 7, accumulate, 0)

    ga.wait_other_far()
    forward(ga, a_sib, (5,))
    for each in to_chips:
        each.wait_recv()
    returned = e_sum[chip].astype(F32)
    for o in range(1, 8):
        returned = returned + e_recv[o].astype(F32)
    returned = returned.reshape(ROWS // 2, CAP, PAIR)
    filled = jnp.concatenate([returned, jnp.zeros((ROWS // 2, PAD - CAP, PAIR), F32)], axis=1)
    g_send[...] = filled.astype(BF16)

    home_first = ch.take(8)
    home_send = ch.take(8)

    def home_copy(i, core):
        dest = (k * 4 + i, chip * 2 + core)
        return pltpu.make_async_remote_copy(
            src_ref=g_send.at[i],
            dst_ref=f_recv.at[r],
            send_sem=send_sems.at[home_send + i * 2 + core],
            recv_sem=recv_sems.at[home_first + r],
            device_id=dest,
            device_id_type=MESH,
        )

    def home_self(i, core):
        return (k * 4 + i == r) & (core == k)

    for i in range(4):
        for core in range(2):
            @pl.when(jnp.logical_not(home_self(i, core)))
            def _(i=i, core=core):
                home_copy(i, core).start()

    @pl.when(r // 4 == k)
    def _():
        f_recv[r] = g_send[r % 4]

    a_sib[(2, 1)].wait_recv()
    down_block(5)
    hg[...] += hidden_block(5)

    def finish(i, carry):
        part = pl.ds(pl.multiple_of(i * 16, 16), 16)
        v = gp_ref[part, :].astype(F32)
        sigma = jax.nn.sigmoid(v)
        grad = hg[part, :]
        upg_ref[part, :] = (grad * (v * sigma)).astype(BF16)
        gpg_ref[part, :] = (grad * up_ref[part, :].astype(F32) * slope_of(v, sigma)).astype(BF16)
        return carry

    lax.fori_loop(0, FFD // 16, finish, 0)

    def home_arrival(source):
        return pltpu.make_async_remote_copy(
            src_ref=g_send.at[0],
            dst_ref=f_recv.at[source],
            send_sem=send_sems.at[home_send],
            recv_sem=recv_sems.at[home_first + source],
            device_id=sib,
            device_id_type=MESH,
        )

    for o in range(1, 8):
        home_arrival((r + o) % 8).wait_recv()

    @pl.when(r // 4 != k)
    def _():
        home_arrival(r).wait_recv()

    halves = f_recv[...].astype(F32).reshape(WIN, 2, PAD, PAIR)
    combined = (halves[:, 0] + halves[:, 1]).reshape(WIN * PAD, PAIR)
    back[...] = jnp.transpose(combined).astype(BF16)
    mig_ref[...] = dot(back[lanes, :], picked[...], NN).astype(BF16)

    def down_arrival(source):
        return pltpu.make_async_remote_copy(
            src_ref=d_send.at[0],
            dst_ref=d_recv.at[source],
            send_sem=send_sems.at[d_first],
            recv_sem=recv_sems.at[d_first + source],
            device_id=sib,
            device_id_type=MESH,
        )

    for o in range(1, 8):
        down_arrival((r + o) % 8).wait_recv()

    def add_down(i, carry):
        part = pl.ds(pl.multiple_of(i * 16, 16), 16)
        total = d_send[r, part].astype(F32)
        for o in range(1, 8):
            total = total + d_recv[(r + o) % 8, part].astype(F32)
        dwg_ref[part, :] = total.astype(BF16)
        return carry

    lax.fori_loop(0, FFD // 16, add_down, 0)

    for each in stores:
        each.wait()
    for each in ch.sent:
        each.wait_send()
    for j in range(8):
        @pl.when(j != r)
        def _(j=j):
            down_copy(j).wait_send()
    for i in range(4):
        for core in range(2):
            @pl.when(jnp.logical_not(home_self(i, core)))
            def _(i=i, core=core):
                home_copy(i, core).wait_send()


def body(
    layer_input, output_grad, gate_pre, up_pre, down_weight,
    route_ids, route_gates, expert_gate, expert_up, expert_down,
):
    vmem = pl.BlockSpec(memory_space=pltpu.VMEM)
    hbm = pl.BlockSpec(memory_space=pl.ANY)

    def shape(*dims, dtype=BF16):
        return jax.ShapeDtypeStruct(dims, dtype)

    def scratch(*dims, dtype=BF16):
        return pltpu.VMEM(dims, dtype)

    outs = pl.pallas_call(
        kernel,
        out_shape=(
            shape(FFD, TOK), shape(FFD, TOK), shape(FFD, PAIR),
            shape(HID, CHIPS * PAIR), shape(HID, CHIPS * PAIR), shape(HID, CHIPS * PAIR),
            shape(FEAT, TOK),
        ),
        in_specs=[vmem] * 4 + [hbm] * 6,
        out_specs=(vmem, vmem, vmem, hbm, hbm, hbm, vmem),
        scratch_shapes=[
            scratch(CHIPS, PAIR, TOK),
            scratch(PAIR, TOK),
            scratch(ROWS, FFD, PAIR),
            scratch(ROWS, FFD, PAIR),
            scratch(ROWS, FFD, PAIR),
            scratch(2, CHIPS, SLOTS, PAIR),
            scratch(HID, CHIPS * PAIR),
            scratch(HID, CHIPS * PAIR),
            scratch(HID, CHIPS * PAIR),
            scratch(CHIPS, SLOTS, PAIR),
            scratch(CHIPS, HALF, PAIR),
            scratch(CHIPS, HALF, PAIR),
            scratch(CHIPS, HALF, PAIR),
            scratch(WIN, PAD, PAIR),
            scratch(ROWS, PAD, PAIR),
            scratch(ROWS // 2, PAD, PAIR),
            scratch(ROWS, PAD, PAIR),
            scratch(WIN * PAD, TOK),
            scratch(FFD, TOK),
            scratch(FFD, TOK, dtype=F32),
            scratch(3, SLOTS, HID, dtype=F32),
            scratch(PAIR, WIN * PAD),
            pltpu.SemaphoreType.DMA((CHANNELS,)),
            pltpu.SemaphoreType.DMA((CHANNELS,)),
            pltpu.SemaphoreType.DMA((16,)),
        ],
        compiler_params=pltpu.CompilerParams(
            collective_id=0, has_side_effects=True, vmem_limit_bytes=63 * 1024 * 1024
        ),
        name="layer_backward",
    )(
        route_ids.T, route_gates.T, gate_pre.T, up_pre.T, output_grad.T, layer_input.T, down_weight,
        expert_gate[0].T, expert_up[0].T, expert_down[0],
    )
    gpg, upg, dwg, gg, ug, dg, mig = outs
    return gpg.T, upg.T, dwg, gg.T[None], ug.T[None], dg[None], mig.T


def solution(mesh):
    in_specs = (
        P("row", "col"),
        P("row", "col"),
        P("row", "col"),
        P("row", "col"),
        P("col", "row"),
        P("row", None),
        P("row", None),
        P("row", None, "col"),
        P("row", None, "col"),
        P("row", "col", None),
    )
    out_specs = (
        P("row", "col"),
        P("row", "col"),
        P("col", "row"),
        P("row", None, "col"),
        P("row", None, "col"),
        P("row", "col", None),
        P("row", "col"),
    )
    return jax.shard_map(body, mesh=mesh, in_specs=in_specs, out_specs=out_specs, check_vma=False)
```

time: 496 us -> 213 us (0.43)
  the two profiles are of different devices: /device:TPU:99 before, /device:TPU:24 now
where the time goes in v1:
time: 213 us
  Pallas kernels  199 us (93%)
  local copies, waits for them, and re-layouts  13.5 us (6%)
    pallas_call x1, Pallas kernels, body(): pl.pallas_call(kernel, out_shape=(shape(FFD, TOK), shape(FFD, TOK), shape...  199 us
    unnamed x15, local copies, waits for them, and re-layouts  13.5 us

profile of v1, /device:TPU:24, one launch (start us, length us, event | category | flops | bytes accessed | tf_op | source)
XLA Modules:
  0.0 212.7 jit_solution(14271876409197651853)
XLA Ops:
  0.6 198.6 %layer_backward.1 = (bf16[304,1024]{1,0:T(8,128)(2,1)}, bf16[304,1024]{1,0:T(8,128)(2,1)}, bf16[304,896]{1,0:T(8,128)(2,1)}, bf16[152,7168]{1,0:T(8,128)(2,1)}, ...) custom-call(s32[2,1024]{1,0:T(2,128)} %bitcast.36, f32[2,1024]{1,0:T(2,128)} %bitcast.37, ...), custom_call_target="tpu_custom_call" | custom-call | tf_op jit(solution)/shard_map/layer_backward/pallas_call | solution.py:542
  199.2 0.0 copy-start.2
  199.2 2.1 copy.24
  201.3 1.9 copy.25
  203.3 1.9 copy.26
  205.1 0.0 copy-done.2
  205.1 0.0 copy-start.1
  205.1 1.3 copy.27
  206.5 1.1 copy-done.1
  207.5 0.0 copy-start
  207.6 1.3 copy.28
  208.9 1.1 copy-done
  210.0 0.0 copy-start.3
  210.0 1.3 copy.29
  211.3 0.5 copy-done.3
  211.8 0.9 copy.30
Async XLA Ops:
  199.2 5.9 %copy-start.2 = (bf16[152,7168]{1,0:T(8,128)(2,1)S(1)}, bf16[152,7168]{1,0:T(8,128)(2,1)}, u32[]{:S(2)}) copy-start(bf16[152,7168]{1,0:T(8,128)(2,1)} %get-tuple-element.17) | copy-start | bytes 6537220
  205.1 2.4 %copy-start.1 = (bf16[152,7168]{1,0:T(8,128)(2,1)S(1)}, bf16[152,7168]{1,0:T(8,128)(2,1)}, u32[]{:S(2)}) copy-start(bf16[152,7168]{1,0:T(8,128)(2,1)} %get-tuple-element.18) | copy-start | bytes 6537220
  207.5 2.4 %copy-start = (bf16[152,7168]{1,0:T(8,128)(2,1)S(1)}, bf16[152,7168]{1,0:T(8,128)(2,1)}, u32[]{:S(2)}) copy-start(bf16[152,7168]{1,0:T(8,128)(2,1)} %get-tuple-element.19) | copy-start | bytes 6537220
  210.0 1.8 copy-start.3

commit v2 on v1

--- a/solution.py
+++ b/solution.py
@@ -74,16 +74,13 @@
     def at(self, delta, flip):
         return self.slot((self.pos + delta) % 4, (self.side + flip) % 2)
 
-    def own(self, src):
+    def own_near(self, src):
         dst = self.at(0, 0)
         self.a = self.ch.go(src, dst, self.right)
         self.b = self.ch.go(src, dst, self.left)
-        self.c = self.ch.go(src, dst, self.across)
-
-    def wait_own(self):
-        self.a.wait_recv()
-        self.b.wait_recv()
-        self.c.wait_recv()
+
+    def own_across(self, src):
+        self.c = self.ch.go(src, self.at(0, 0), self.across)
 
     def _far(self, flip):
         lo, hi = pl.ds(0, self.cut), pl.ds(self.cut, self.size - self.cut)
@@ -93,33 +90,36 @@
             self.ch.go(from_right.at[hi], from_right.at[hi], self.left),
         )
 
+    def near_done(self):
+        self.a.wait_recv()
+        self.b.wait_recv()
+
     def far(self):
         self.d = self._far(0)
 
-    def wait_far(self):
-        self.d[0].wait_recv()
-        self.d[1].wait_recv()
-
-    def other(self):
+    def across_done(self):
+        self.c.wait_recv()
         src = self.at(0, 1)
         self.e = (self.ch.go(src, src, self.right), self.ch.go(src, src, self.left))
 
-    def wait_other(self):
-        self.e[0].wait_recv()
-        self.e[1].wait_recv()
-
-    def other_far(self):
+    def far_done(self):
+        for each in self.d:
+            each.wait_recv()
+
+    def other_done(self):
+        for each in self.e:
+            each.wait_recv()
         self.f = self._far(1)
 
-    def wait_other_far(self):
-        self.f[0].wait_recv()
-        self.f[1].wait_recv()
+    def all_done(self):
+        for each in self.f:
+            each.wait_recv()
 
 
 def kernel(
     ids_ref, gates_ref, gp_ref, up_ref, og, li, dw, wg, wu, wd,
     gpg_ref, upg_ref, dwg_ref, gg, ug, dg, mig_ref,
-    panel, li_pair, dw_all, d_send, d_recv, rows, w_gate, w_up, w_down,
+    panel, li_pair, dw_all, d_send, y_recv, z_recv, rows, w_gate, w_up, w_down,
     e_part, e_sib, e_sum, e_recv, c_send, c_recv, g_send, f_recv,
     picked, hidden, hg, mids, back, send_sems, recv_sems, local_sems,
 ):
@@ -182,8 +182,8 @@
     own_slot = panel_slot(x, yh)
     sib_og = ch.go(og, own_slot, sib)
     sib_li = ch.go(li, li_slot, sib)
-    ga.own(og)
-    gb.own(dw)
+    ga.own_near(og)
+    ga.own_across(og)
     local = [
         pltpu.make_async_copy(og, own_slot, local_sems.at[0]),
         pltpu.make_async_copy(li, li_slot, local_sems.at[1]),
@@ -239,6 +239,8 @@
     keep = pltpu.make_async_copy(c_send.at[r // 2], c_recv.at[r], local_sems.at[6])
     keep.start()
 
+    gb.own_near(dw)
+
     def hide(i, carry):
         part = pl.ds(pl.multiple_of(i * 16, 16), 16)
         v = gp_ref[part, :].astype(F32)
@@ -246,6 +248,72 @@
         return carry
 
     lax.fori_loop(0, FFD // 16, hide, 0)
+
+    y_first = ch.take(4)
+    y_out = ch.take(8)
+    z_first = ch.take(4)
+    z_out = ch.take(4)
+
+    def chip_at(o):
+        return chip_of((x + o // 2) % 4, (yh + o % 2) % 2)
+
+    def y_copy(j):
+        return pltpu.make_async_remote_copy(
+            src_ref=d_send.at[j],
+            dst_ref=y_recv.at[j % 4],
+            send_sem=send_sems.at[y_out + j],
+            recv_sem=recv_sems.at[y_first + j % 4],
+            device_id=row_dev(row_of(1 - yl, z)),
+            device_id_type=MESH,
+        )
+
+    def z_copy(to):
+        return pltpu.make_async_remote_copy(
+            src_ref=d_send.at[row_of(yl, to)],
+            dst_ref=z_recv.at[z],
+            send_sem=send_sems.at[z_out + to],
+            recv_sem=recv_sems.at[z_first + z],
+            device_id=row_dev(row_of(yl, to)),
+            device_id_type=MESH,
+        )
+
+    def z_arrival(source):
+        return pltpu.make_async_remote_copy(
+            src_ref=d_send.at[0],
+            dst_ref=z_recv.at[source],
+            send_sem=send_sems.at[z_out],
+            recv_sem=recv_sems.at[z_first + source],
+            device_id=sib,
+            device_id_type=MESH,
+        )
+
+    def down_block(o):
+        j = chip_at(o)
+        d_send[j] = dot(hidden[...], panel[j], NT).astype(BF16)
+
+        @pl.when(j // 4 != yl)
+        def _():
+            y_copy(j).start()
+
+    def down_join(o):
+        j = chip_at(o)
+        to = j % 4
+
+        @pl.when(j // 4 == yl)
+        def _():
+            y_copy(j).wait_recv()
+
+            def add(i, carry):
+                part = pl.ds(pl.multiple_of(i * 16, 16), 16)
+                d_send[j, part] = (d_send[j, part].astype(F32) + y_recv[to, part].astype(F32)).astype(BF16)
+                return carry
+
+            lax.fori_loop(0, FFD // 16, add, 0)
+
+            @pl.when(to != z)
+            def _():
+                z_copy(to).start()
+
 
     for each in to_experts:
         each.wait_recv()
@@ -253,91 +321,107 @@
     packed = c_recv[...].astype(F32)[:, :CAP, :].reshape(SLOTS, PAIR).astype(BF16)
     rows[k, chip] = packed
     gc_own = gc.at(0, 0)
-    c_sib = {(0, 0): ch.go(gc_own, gc_own, sib)}
-    gc.own(gc_own)
-
-    d_first = ch.take(8)
-
-    def down_block(o):
-        j = chip_of((x + o // 2) % 4, (yh + o % 2) % 2)
-        d_send[j] = dot(hidden[...], panel[j], NT).astype(BF16)
-
-        @pl.when(j != r)
-        def _():
-            down_copy(j).start()
-
-    def down_copy(j):
-        return pltpu.make_async_remote_copy(
-            src_ref=d_send.at[j],
-            dst_ref=d_recv.at[r],
-            send_sem=send_sems.at[d_first + j],
-            recv_sem=recv_sems.at[d_first + r],
-            device_id=row_dev(j),
-            device_id_type=MESH,
-        )
+    c_sib = {0: ch.go(gc_own, gc_own, sib)}
+    gc.own_near(gc_own)
+    gc.own_across(gc_own)
 
     def forward(gather, kept, offsets):
         for o in offsets:
             slot = gather.at(o // 2, o % 2)
-            kept[(o // 2, o % 2)] = ch.go(slot, slot, sib)
-
-    down_block(0)
-
-    a_sib = {}
-    ga.wait_own()
-    forward(ga, a_sib, (1, 2, 6))
-    ga.far()
-    gb.wait_own()
-    gb.far()
-    gb.other()
-
-    gc.wait_own()
-    gc.other()
-    gc.far()
-    forward(gc, c_sib, (1, 2, 6))
-
-    for o in (1, 2, 6):
-        a_sib[(o // 2, o % 2)].wait_recv()
-
-    def near(i, carry):
-        down_block(jnp.where(i == 0, 1, jnp.where(i == 1, 2, 6)))
-        return carry
-
-    lax.fori_loop(0, 3, near, 0)
-
-    gc.wait_other()
-    gc.other_far()
-    gc.wait_far()
-    forward(gc, c_sib, (3, 4, 7))
-    ga.wait_far()
-    forward(ga, a_sib, (4,))
-    ga.other()
-    gb.wait_other()
-    gb.other_far()
-    gb.wait_far()
-    gc.wait_other_far()
-    forward(gc, c_sib, (5,))
-    a_sib[(2, 0)].wait_recv()
-    down_block(4)
-    for each in c_sib.values():
-        each.wait_recv()
-    for each in local[3:]:
-        each.wait()
-
-    mids[...] = jnp.zeros_like(mids)
+            kept[o] = ch.go(slot, slot, sib)
 
     def lanes_of(i):
         return pl.ds(pl.multiple_of(i * PAIR, 128), PAIR)
 
-    def enter(i, carry):
+    def enter(o):
+        i = chip_at(o)
         part = lanes_of(i)
         taken = rows[0, i]
         mids[0] += dot(taken, w_gate[:, part], NT)
         mids[1] += dot(taken, w_up[:, part], NT)
         mids[2] += dot(rows[1, i], w_down[:, part], NT)
-        return carry
-
-    lax.fori_loop(0, CHIPS, enter, 0)
+
+    def hidden_block(o):
+        j = chip_at(o)
+        hg[...] += dot(dw_all[j], panel[j], NN)
+
+    def near_offset(i):
+        return jnp.where(i == 0, 1, jnp.where(i == 1, 2, 6))
+
+    def over(count, what, offset):
+        def step(i, carry):
+            what(offset(i))
+            return carry
+
+        lax.fori_loop(0, count, step, 0)
+
+    mids[...] = jnp.zeros_like(mids)
+    hg[...] = jnp.zeros_like(hg)
+
+    a_sib = {}
+    for each in local[3:]:
+        each.wait()
+    c_sib[0].wait_recv()
+    enter(0)
+    ga.near_done()
+    forward(ga, a_sib, (2, 6))
+    ga.far()
+    ga.across_done()
+    forward(ga, a_sib, (1,))
+    gb.own_across(dw)
+    down_block(0)
+    for o in (1, 2, 6):
+        a_sib[o].wait_recv()
+    over(3, down_block, near_offset)
+    gb.near_done()
+    gb.far()
+    gc.near_done()
+    forward(gc, c_sib, (2, 6))
+    gc.across_done()
+    gc.far()
+    forward(gc, c_sib, (1,))
+    for o in (1, 2, 6):
+        c_sib[o].wait_recv()
+    over(3, enter, near_offset)
+    gb.across_done()
+    down_join(0)
+    over(3, down_join, near_offset)
+
+    ga.far_done()
+    forward(ga, a_sib, (4,))
+    a_sib[4].wait_recv()
+    down_block(4)
+    gc.far_done()
+    forward(gc, c_sib, (4,))
+    gb.far_done()
+    gb.other_done()
+    c_sib[4].wait_recv()
+    enter(4)
+    ga.other_done()
+    forward(ga, a_sib, (3, 7))
+    gc.other_done()
+    forward(gc, c_sib, (3, 7))
+    for o in (3, 7):
+        a_sib[o].wait_recv()
+    over(2, down_block, lambda i: 3 + 4 * i)
+    down_join(4)
+    for o in (3, 7):
+        c_sib[o].wait_recv()
+    over(2, enter, lambda i: 3 + 4 * i)
+
+    ga.all_done()
+    forward(ga, a_sib, (5,))
+    a_sib[5].wait_recv()
+    down_block(5)
+    over(2, down_join, lambda i: 3 + 4 * i)
+    gb.all_done()
+    local[2].wait()
+    over(4, hidden_block, lambda i: i)
+    gc.all_done()
+    forward(gc, c_sib, (5,))
+    c_sib[5].wait_recv()
+    enter(5)
+
     gate_value, up_value, inner_grad = mids[0], mids[1], mids[2]
     sigma = jax.nn.sigmoid(gate_value)
     active = gate_value * sigma
@@ -345,32 +429,38 @@
     up_local = (inner_grad * active).astype(BF16)
     gate_local = (inner_grad * up_value * slope_of(gate_value, sigma)).astype(BF16)
 
-    def leave(i, carry):
+    mine = pl.ds(pl.multiple_of(k * HALF, HALF), HALF)
+    theirs = pl.ds(pl.multiple_of((1 - k) * HALF, HALF), HALF)
+    between = ch.take(8)
+    outward = ch.take(8)
+
+    def to_sib(o):
+        return ch.copy(e_part.at[chip_at(o), theirs], e_sib.at[o], sib, between + o)
+
+    def to_chip(o):
+        x_, yh_ = (x + o // 2) % 4, (yh + o % 2) % 2
+        return ch.copy(e_sum.at[o], e_recv.at[o], col_dev(x_, yh_), outward + o)
+
+    def leave(o):
+        i = chip_at(o)
         part = lanes_of(i)
         total = dot(gate_local, w_gate[:, part], NN) + dot(up_local, w_up[:, part], NN)
         e_part[i] = total.astype(BF16)
+        to_sib(o).start()
+
+    def join(o):
+        to_sib(o).wait_recv()
+        e_sum[o] = (e_part[chip_at(o), mine].astype(F32) + e_sib[o].astype(F32)).astype(BF16)
+
+    def part_out(i, carry):
+        leave((i + 1) % 8)
+        join(i)
+        to_chip(i).start()
         return carry
 
-    lax.fori_loop(0, CHIPS, leave, 0)
-
-    mine = pl.ds(pl.multiple_of(k * HALF, HALF), HALF)
-    theirs = pl.ds(pl.multiple_of((1 - k) * HALF, HALF), HALF)
-    between = ch.go(e_part.at[:, theirs], e_sib, sib)
-
-    ga.wait_other()
-    ga.other_far()
-    forward(ga, a_sib, (3, 7))
-    between.wait_recv()
-
-    def add_sib(i, carry):
-        e_sum[i] = (e_part[i, mine].astype(F32) + e_sib[i].astype(F32)).astype(BF16)
-        return carry
-
-    lax.fori_loop(0, CHIPS, add_sib, 0)
-    to_chips = []
-    for o in range(1, 8):
-        x_, yh_ = (x + o // 2) % 4, (yh + o % 2) % 2
-        to_chips.append(ch.go(e_sum.at[chip_of(x_, yh_)], e_recv.at[o], col_dev(x_, yh_)))
+    leave(1)
+    lax.fori_loop(1, 8, part_out, 0)
+    join(0)
 
     def grads(i, carry):
         part = lanes_of(i)
@@ -380,6 +470,7 @@
         w_down[:, part] = dot(inner, rows[1, i], TN).astype(BF16)
         return carry
 
+    down_join(5)
     lax.fori_loop(0, CHIPS, grads, 0)
     stores = [
         pltpu.make_async_copy(w_gate, gg, local_sems.at[7]),
@@ -389,35 +480,11 @@
     for each in stores:
         each.start()
 
-    a_sib[(1, 1)].wait_recv()
-    a_sib[(3, 1)].wait_recv()
-
-    def partner(i, carry):
-        down_block(jnp.where(i == 0, 3, 7))
-        return carry
-
-    lax.fori_loop(0, 2, partner, 0)
-
-    gb.wait_other_far()
-    local[2].wait()
-
-    def hidden_block(o):
-        j = chip_of((x + o // 2) % 4, (yh + o % 2) % 2)
-        return dot(dw_all[j], panel[j], NN)
-
-    hg[...] = hidden_block(0)
-
-    def accumulate(i, carry):
-        hg[...] += hidden_block(jnp.where(i < 5, i, i + 1))
-        return carry
-
-    lax.fori_loop(1, 7, accumulate, 0)
-
-    ga.wait_other_far()
-    forward(ga, a_sib, (5,))
-    for each in to_chips:
-        each.wait_recv()
-    returned = e_sum[chip].astype(F32)
+    over(4, hidden_block, lambda i: 4 + i)
+
+    for o in range(1, 8):
+        to_chip(o).wait_recv()
+    returned = e_sum[0].astype(F32)
     for o in range(1, 8):
         returned = returned + e_recv[o].astype(F32)
     returned = returned.reshape(ROWS // 2, CAP, PAIR)
@@ -451,10 +518,6 @@
     def _():
         f_recv[r] = g_send[r % 4]
 
-    a_sib[(2, 1)].wait_recv()
-    down_block(5)
-    hg[...] += hidden_block(5)
-
     def finish(i, carry):
         part = pl.ds(pl.multiple_of(i * 16, 16), 16)
         v = gp_ref[part, :].astype(F32)
@@ -488,24 +551,14 @@
     back[...] = jnp.transpose(combined).astype(BF16)
     mig_ref[...] = dot(back[lanes, :], picked[...], NN).astype(BF16)
 
-    def down_arrival(source):
-        return pltpu.make_async_remote_copy(
-            src_ref=d_send.at[0],
-            dst_ref=d_recv.at[source],
-            send_sem=send_sems.at[d_first],
-            recv_sem=recv_sems.at[d_first + source],
-            device_id=sib,
-            device_id_type=MESH,
-        )
-
-    for o in range(1, 8):
-        down_arrival((r + o) % 8).wait_recv()
+    for o in range(1, 4):
+        z_arrival((z + o) % 4).wait_recv()
 
     def add_down(i, carry):
         part = pl.ds(pl.multiple_of(i * 16, 16), 16)
         total = d_send[r, part].astype(F32)
-        for o in range(1, 8):
-            total = total + d_recv[(r + o) % 8, part].astype(F32)
+        for o in range(1, 4):
+            total = total + z_recv[(z + o) % 4, part].astype(F32)
         dwg_ref[part, :] = total.astype(BF16)
         return carry
 
@@ -515,15 +568,64 @@
         each.wait()
     for each in ch.sent:
         each.wait_send()
+    for o in range(8):
+        to_sib(o).wait_send()
+        if o:
+            to_chip(o).wait_send()
     for j in range(8):
-        @pl.when(j != r)
+        @pl.when(j // 4 != yl)
         def _(j=j):
-            down_copy(j).wait_send()
+            y_copy(j).wait_send()
+    for to in range(4):
+        @pl.when(to != z)
+        def _(to=to):
+            z_copy(to).wait_send()
     for i in range(4):
         for core in range(2):
             @pl.when(jnp.logical_not(home_self(i, core)))
             def _(i=i, core=core):
                 home_copy(i, core).wait_send()
+
+
+def pieces(shape):
+    width = shape[1] // 2 if shape[1] > 2 * TOK else shape[1]
+    return [pl.ds(at, width) for at in range(0, shape[1], width)]
+
+
+def place_kernel(*refs):
+    count = (len(refs) - 2) // 3
+    read_sems, write_sems = refs[-2:]
+    pairs = []
+    for src, dst, held in zip(refs[:count], refs[count : 2 * count], refs[2 * count : 3 * count]):
+        for part in pieces(src.shape):
+            n = len(pairs)
+            pairs.append((
+                pltpu.make_async_copy(src.at[:, part], held.at[:, part], read_sems.at[n]),
+                pltpu.make_async_copy(held.at[:, part], dst.at[:, part], write_sems.at[n]),
+            ))
+    for read, _ in pairs:
+        read.start()
+    for read, write in pairs:
+        read.wait()
+        write.start()
+    for _, write in pairs:
+        write.wait()
+
+
+def place(arrays):
+    hbm = pl.BlockSpec(memory_space=pl.ANY)
+    count = len(arrays)
+    total = sum(len(pieces(a.shape)) for a in arrays)
+    return pl.pallas_call(
+        place_kernel,
+        out_shape=tuple(jax.ShapeDtypeStruct(a.shape, a.dtype) for a in arrays),
+        in_specs=[hbm] * count,
+        out_specs=(hbm,) * count,
+        scratch_shapes=[pltpu.VMEM(a.shape, a.dtype) for a in arrays]
+        + [pltpu.SemaphoreType.DMA((total,)), pltpu.SemaphoreType.DMA((total,))],
+        compiler_params=pltpu.CompilerParams(vmem_limit_bytes=63 * 1024 * 1024),
+        name="place_results",
+    )(*arrays)
 
 
 def body(
@@ -553,7 +655,8 @@
             scratch(PAIR, TOK),
             scratch(ROWS, FFD, PAIR),
             scratch(ROWS, FFD, PAIR),
-            scratch(ROWS, FFD, PAIR),
+            scratch(ROWS // 2, FFD, PAIR),
+            scratch(ROWS // 2, FFD, PAIR),
             scratch(2, CHIPS, SLOTS, PAIR),
             scratch(HID, CHIPS * PAIR),
             scratch(HID, CHIPS * PAIR),
@@ -583,7 +686,7 @@
         route_ids.T, route_gates.T, gate_pre.T, up_pre.T, output_grad.T, layer_input.T, down_weight,
         expert_gate[0].T, expert_up[0].T, expert_down[0],
     )
-    gpg, upg, dwg, gg, ug, dg, mig = outs
+    gpg, upg, dwg, gg, ug, dg, mig = place(outs)
     return gpg.T, upg.T, dwg, gg.T[None], ug.T[None], dg[None], mig.T
 
 

time: 213 us -> 173 us (0.81)
  the two profiles are of different devices: /device:TPU:24 before, /device:TPU:25 now
where the time goes in v2:
time: 173 us
  Pallas kernels  173 us (100%)
    pallas_call x1, Pallas kernels, body(): pl.pallas_call(kernel, out_shape=(shape(FFD, TOK), shape(FFD, TOK), shape...  165 us
    pallas_call x1, Pallas kernels, place(): pl.pallas_call(place_kernel, out_shape=tuple((jax.ShapeDtypeStruct(a.shap...  7.36 us

profile of v2, /device:TPU:25, one launch (start us, length us, event | category | flops | bytes accessed | tf_op | source)
XLA Modules:
  0.0 173.3 jit_solution(660872731286226353)
XLA Ops:
  0.6 165.3 %layer_backward.1 = (bf16[304,1024]{1,0:T(8,128)(2,1)}, bf16[304,1024]{1,0:T(8,128)(2,1)}, bf16[304,896]{1,0:T(8,128)(2,1)}, bf16[152,7168]{1,0:T(8,128)(2,1)}, ...) custom-call(s32[2,1024]{1,0:T(2,128)} %bitcast.30, f32[2,1024]{1,0:T(2,128)} %bitcast.31, ...), custom_call_target="tpu_custom_call" | custom-call | tf_op jit(solution)/shard_map/layer_backward/pallas_call | solution.py:644
  166.0 7.4 %place_results.1 = (bf16[304,1024]{1,0:T(8,128)(2,1)}, bf16[304,1024]{1,0:T(8,128)(2,1)}, bf16[304,896]{1,0:T(8,128)(2,1)}, bf16[152,7168]{1,0:T(8,128)(2,1)}, b...) custom-call(bf16[304,1024]{1,0:T(8,128)(2,1)} %get-tuple-element.21.refs_0_, ...), custom_call_target="tpu_custom_call" | custom-call | tf_op jit(solution)/shard_map/place_results/pallas_call | solution.py:619

commit v3 on v2

--- a/solution.py
+++ b/solution.py
@@ -62,7 +62,7 @@
         return made
 
 
-CHANNELS = 128
+CHANNELS = 160
 
 
 class RingPair:
@@ -99,6 +99,8 @@
 
     def across_done(self):
         self.c.wait_recv()
+
+    def other(self):
         src = self.at(0, 1)
         self.e = (self.ch.go(src, src, self.right), self.ch.go(src, src, self.left))
 
@@ -109,7 +111,13 @@
     def other_done(self):
         for each in self.e:
             each.wait_recv()
+
+    def other_far(self):
         self.f = self._far(1)
+
+    def far_across(self):
+        src = self.at(2, 0)
+        self.f = (self.ch.go(src, src, self.across),)
 
     def all_done(self):
         for each in self.f:
@@ -117,9 +125,9 @@
 
 
 def kernel(
-    ids_ref, gates_ref, gp_ref, up_ref, og, li, dw, wg, wu, wd,
-    gpg_ref, upg_ref, dwg_ref, gg, ug, dg, mig_ref,
-    panel, li_pair, dw_all, d_send, y_recv, z_recv, rows, w_gate, w_up, w_down,
+    ids_ref, gates_ref, gp, up, og, li, dw, wg, wu, wd,
+    gpg, upg, dwg, gg, ug, dg, mig,
+    gp_ref, up_ref, panel, li_pair, dw_all, d_send, d_recv, y_recv, y_last, rows, w_gate, w_up, w_down,
     e_part, e_sib, e_sum, e_recv, c_send, c_recv, g_send, f_recv,
     picked, hidden, hg, mids, back, send_sems, recv_sems, local_sems,
 ):
@@ -156,8 +164,6 @@
             barrier, inc=1, device_id=((r + o) % 8, chip * 2 + (1 - k)), device_id_type=MESH
         )
         greeted += 1
-    pl.semaphore_wait(barrier, greeted)
-
     ch = Channels(send_sems, recv_sems)
     lanes = pl.ds(pl.multiple_of(k * FEAT, FEAT), FEAT)
 
@@ -170,20 +176,8 @@
     def dw_slot(z_, yl_):
         return dw_all.at[row_of(yl_, z_)]
 
-    x_right, x_left, y_across = col_dev((x + 1) % 4, yh), col_dev((x + 3) % 4, yh), col_dev(x, 1 - yh)
-    ga = RingPair(ch, panel_slot, FEAT // 2, FEAT, x, yh, x_right, x_left, y_across)
-    gc = RingPair(ch, rows_slot, HALF, SLOTS, x, yh, x_right, x_left, y_across)
-    gb = RingPair(
-        ch, dw_slot, 160, FFD, z, yl,
-        row_dev(row_of(yl, (z + 1) % 4)), row_dev(row_of(yl, (z + 3) % 4)), row_dev(row_of(1 - yl, z)),
-    )
-
     li_slot = li_pair.at[lanes]
     own_slot = panel_slot(x, yh)
-    sib_og = ch.go(og, own_slot, sib)
-    sib_li = ch.go(li, li_slot, sib)
-    ga.own_near(og)
-    ga.own_across(og)
     local = [
         pltpu.make_async_copy(og, own_slot, local_sems.at[0]),
         pltpu.make_async_copy(li, li_slot, local_sems.at[1]),
@@ -191,6 +185,8 @@
         pltpu.make_async_copy(wg, w_gate, local_sems.at[3]),
         pltpu.make_async_copy(wu, w_up, local_sems.at[4]),
         pltpu.make_async_copy(wd, w_down, local_sems.at[5]),
+        pltpu.make_async_copy(gp, gp_ref, local_sems.at[10]),
+        pltpu.make_async_copy(up, up_ref, local_sems.at[11]),
     ]
     for each in local:
         each.start()
@@ -217,13 +213,34 @@
         weights.append(jnp.sum(mine * gate_of[e : e + 1, :], axis=1, keepdims=True))
     weights = jnp.concatenate(weights, axis=0)
 
+    pl.semaphore_wait(barrier, greeted)
+
+    x_right, x_left, y_across = col_dev((x + 1) % 4, yh), col_dev((x + 3) % 4, yh), col_dev(x, 1 - yh)
+    ga = RingPair(ch, panel_slot, FEAT // 2, FEAT, x, yh, x_right, x_left, y_across)
+    gc = RingPair(ch, rows_slot, HALF, SLOTS, x, yh, x_right, x_left, y_across)
+    gb = RingPair(
+        ch, dw_slot, 160, FFD, z, yl,
+        row_dev(row_of(yl, (z + 1) % 4)), row_dev(row_of(yl, (z + 3) % 4)), row_dev(row_of(1 - yl, z)),
+    )
+
     local[0].wait()
     local[1].wait()
+    sib_og = ch.copy(own_slot, own_slot, sib)
+    sib_li = ch.copy(li_slot, li_slot, sib)
+
+    @pl.when(k == 1)
+    def _():
+        sib_li.start()
+
+    sib_og.start()
+    ch.sent.append(sib_og)
+    ga.own_near(own_slot)
+    ga.own_across(own_slot)
     sib_og.wait_recv()
-    sib_li.wait_recv()
 
     @pl.when(k == 0)
     def _():
+        sib_li.wait_recv()
         chosen = dot(picked[...], li_pair[...], NT)
         c_send[...] = chosen.astype(BF16).reshape(WIN, PAD, PAIR)
 
@@ -239,7 +256,11 @@
     keep = pltpu.make_async_copy(c_send.at[r // 2], c_recv.at[r], local_sems.at[6])
     keep.start()
 
-    gb.own_near(dw)
+    local[2].wait()
+    gb.own_near(dw_slot(z, yl))
+
+    local[6].wait()
+    local[7].wait()
 
     def hide(i, carry):
         part = pl.ds(pl.multiple_of(i * 16, 16), 16)
@@ -249,71 +270,113 @@
 
     lax.fori_loop(0, FFD // 16, hide, 0)
 
+    d_first = ch.take(16)
+    d_out = ch.take(16)
     y_first = ch.take(4)
-    y_out = ch.take(8)
-    z_first = ch.take(4)
-    z_out = ch.take(4)
+    y_out = ch.take(16)
+    cuts = (pl.ds(0, 160), pl.ds(160, FFD - 160))
 
     def chip_at(o):
         return chip_of((x + o // 2) % 4, (yh + o % 2) % 2)
 
-    def y_copy(j):
+    def z_copy(j, p):
+        to = (j // 4) * 4 + z
         return pltpu.make_async_remote_copy(
-            src_ref=d_send.at[j],
-            dst_ref=y_recv.at[j % 4],
-            send_sem=send_sems.at[y_out + j],
-            recv_sem=recv_sems.at[y_first + j % 4],
+            src_ref=d_send.at[j, cuts[p]],
+            dst_ref=d_recv.at[to, cuts[p]],
+            send_sem=send_sems.at[d_out + j * 2 + p],
+            recv_sem=recv_sems.at[d_first + to * 2 + p],
+            device_id=row_dev(row_of(yl, j % 4)),
+            device_id_type=MESH,
+        )
+
+    def z_arrival(side, source, p):
+        to = side * 4 + source
+        return pltpu.make_async_remote_copy(
+            src_ref=d_send.at[0, cuts[p]],
+            dst_ref=d_recv.at[to, cuts[p]],
+            send_sem=send_sems.at[d_out + p],
+            recv_sem=recv_sems.at[d_first + to * 2 + p],
+            device_id=sib,
+            device_id_type=MESH,
+        )
+
+    def y_copy(j, p):
+        to = (j % 4) // 2
+        return pltpu.make_async_remote_copy(
+            src_ref=d_send.at[j, cuts[p]],
+            dst_ref=y_recv.at[to, cuts[p]],
+            send_sem=send_sems.at[y_out + j * 2 + p],
+            recv_sem=recv_sems.at[y_first + to * 2 + p],
             device_id=row_dev(row_of(1 - yl, z)),
             device_id_type=MESH,
         )
 
-    def z_copy(to):
-        return pltpu.make_async_remote_copy(
-            src_ref=d_send.at[row_of(yl, to)],
-            dst_ref=z_recv.at[z],
-            send_sem=send_sems.at[z_out + to],
-            recv_sem=recv_sems.at[z_first + z],
-            device_id=row_dev(row_of(yl, to)),
-            device_id_type=MESH,
-        )
-
-    def z_arrival(source):
-        return pltpu.make_async_remote_copy(
-            src_ref=d_send.at[0],
-            dst_ref=z_recv.at[source],
-            send_sem=send_sems.at[z_out],
-            recv_sem=recv_sems.at[z_first + source],
-            device_id=sib,
-            device_id_type=MESH,
-        )
-
-    def down_block(o):
+    def down_z(o):
         j = chip_at(o)
         d_send[j] = dot(hidden[...], panel[j], NT).astype(BF16)
 
+        @pl.when(j % 4 != z)
+        def _():
+            for p in range(2):
+                z_copy(j, p).start()
+
+    def down_y(o):
+        j = chip_at(o)
+        d_send[j] = dot(hidden[...], panel[j], NT).astype(BF16)
+
         @pl.when(j // 4 != yl)
         def _():
-            y_copy(j).start()
+            for p in range(2):
+                y_copy(j, p).start()
 
     def down_join(o):
         j = chip_at(o)
-        to = j % 4
 
         @pl.when(j // 4 == yl)
         def _():
-            y_copy(j).wait_recv()
-
-            def add(i, carry):
+            for p in range(2):
+                y_copy(j, p).wait_recv()
+
+                def add(i, carry, p=p):
+                    part = pl.ds(pl.multiple_of(p * 160 + i * 16, 16), 16)
+                    total = d_send[j, part].astype(F32) + y_recv[(j % 4) // 2, part].astype(F32)
+                    d_send[j, part] = total.astype(BF16)
+                    return carry
+
+                lax.fori_loop(0, 10 - p, add, 0)
+
+                @pl.when(j % 4 != z)
+                def _(p=p):
+                    z_copy(j, p).start()
+
+    def sum_z(side, part, j):
+        total = d_send[j, part].astype(F32)
+        for o in range(1, 4):
+            total = total + d_recv[side * 4 + (z + o) % 4, part].astype(F32)
+        return total
+
+    def wait_z(side):
+        for o in range(1, 4):
+            for p in range(2):
+                z_arrival(side, (z + o) % 4, p).wait_recv()
+
+    across_row = row_of(1 - yl, z)
+    z_mode = (z % 2 == yh) | (z // 2 == x % 2)
+    y_final = ch.copy(d_send.at[across_row], y_last, row_dev(across_row))
+
+    def down_cross():
+        @pl.when(z_mode)
+        def _():
+            wait_z(1 - yl)
+
+            def add_cross(i, carry):
                 part = pl.ds(pl.multiple_of(i * 16, 16), 16)
-                d_send[j, part] = (d_send[j, part].astype(F32) + y_recv[to, part].astype(F32)).astype(BF16)
+                d_send[across_row, part] = sum_z(1 - yl, part, across_row).astype(BF16)
                 return carry
 
-            lax.fori_loop(0, FFD // 16, add, 0)
-
-            @pl.when(to != z)
-            def _():
-                z_copy(to).start()
-
+            lax.fori_loop(0, FFD // 16, add_cross, 0)
+            y_final.start()
 
     for each in to_experts:
         each.wait_recv()
@@ -359,66 +422,66 @@
     hg[...] = jnp.zeros_like(hg)
 
     a_sib = {}
-    for each in local[3:]:
+    down_z(0)
+    for each in local[3:6]:
         each.wait()
     c_sib[0].wait_recv()
     enter(0)
     ga.near_done()
+    ga.far()
     forward(ga, a_sib, (2, 6))
-    ga.far()
     ga.across_done()
+    ga.other()
     forward(ga, a_sib, (1,))
-    gb.own_across(dw)
-    down_block(0)
-    for o in (1, 2, 6):
-        a_sib[o].wait_recv()
-    over(3, down_block, near_offset)
+    gb.own_across(dw_slot(z, yl))
     gb.near_done()
     gb.far()
     gc.near_done()
     forward(gc, c_sib, (2, 6))
     gc.across_done()
-    gc.far()
     forward(gc, c_sib, (1,))
+    for o in (2, 6):
+        a_sib[o].wait_recv()
+    over(2, down_z, lambda i: 2 + 4 * i)
+    a_sib[1].wait_recv()
+    down_z(1)
     for o in (1, 2, 6):
         c_sib[o].wait_recv()
     over(3, enter, near_offset)
+
+    ga.far_done()
+    ga.far_across()
+    gc.other()
+    gc.far()
+    forward(ga, a_sib, (4,))
     gb.across_done()
-    down_join(0)
-    over(3, down_join, near_offset)
-
-    ga.far_done()
-    forward(ga, a_sib, (4,))
+    gb.other()
     a_sib[4].wait_recv()
-    down_block(4)
+    down_z(4)
     gc.far_done()
     forward(gc, c_sib, (4,))
     gb.far_done()
-    gb.other_done()
     c_sib[4].wait_recv()
     enter(4)
+    gc.other_done()
+    gc.other_far()
+    forward(gc, c_sib, (3, 7))
     ga.other_done()
     forward(ga, a_sib, (3, 7))
-    gc.other_done()
-    forward(gc, c_sib, (3, 7))
+    gb.other_done()
+    gb.other_far()
     for o in (3, 7):
         a_sib[o].wait_recv()
-    over(2, down_block, lambda i: 3 + 4 * i)
-    down_join(4)
+    over(2, down_y, lambda i: 3 + 4 * i)
     for o in (3, 7):
         c_sib[o].wait_recv()
     over(2, enter, lambda i: 3 + 4 * i)
-
     ga.all_done()
     forward(ga, a_sib, (5,))
-    a_sib[5].wait_recv()
-    down_block(5)
-    over(2, down_join, lambda i: 3 + 4 * i)
-    gb.all_done()
-    local[2].wait()
-    over(4, hidden_block, lambda i: i)
     gc.all_done()
     forward(gc, c_sib, (5,))
+    a_sib[5].wait_recv()
+    down_z(5)
     c_sib[5].wait_recv()
     enter(5)
 
@@ -453,34 +516,20 @@
         e_sum[o] = (e_part[chip_at(o), mine].astype(F32) + e_sib[o].astype(F32)).astype(BF16)
 
     def part_out(i, carry):
-        leave((i + 1) % 8)
-        join(i)
-        to_chip(i).start()
+        leave(6 - i)
+        join(7 - i)
+        to_chip(7 - i).start()
         return carry
 
-    leave(1)
-    lax.fori_loop(1, 8, part_out, 0)
+    leave(7)
+    lax.fori_loop(0, 7, part_out, 0)
     join(0)
 
-    def grads(i, carry):
-        part = lanes_of(i)
-        taken = rows[0, i]
-        w_gate[:, part] = dot(gate_local, taken, TN).astype(BF16)
-        w_up[:, part] = dot(up_local, taken, TN).astype(BF16)
-        w_down[:, part] = dot(inner, rows[1, i], TN).astype(BF16)
-        return carry
-
-    down_join(5)
-    lax.fori_loop(0, CHIPS, grads, 0)
-    stores = [
-        pltpu.make_async_copy(w_gate, gg, local_sems.at[7]),
-        pltpu.make_async_copy(w_up, ug, local_sems.at[8]),
-        pltpu.make_async_copy(w_down, dg, local_sems.at[9]),
-    ]
-    for each in stores:
-        each.start()
-
-    over(4, hidden_block, lambda i: 4 + i)
+    over(2, down_join, lambda i: 3 + 4 * i)
+
+    gb.all_done()
+    over(4, hidden_block, lambda i: i)
+    down_cross()
 
     for o in range(1, 8):
         to_chip(o).wait_recv()
@@ -518,16 +567,40 @@
     def _():
         f_recv[r] = g_send[r % 4]
 
+    def grads(i, carry):
+        part = lanes_of(i)
+        taken = rows[0, i]
+        w_gate[:, part] = dot(gate_local, taken, TN).astype(BF16)
+        w_up[:, part] = dot(up_local, taken, TN).astype(BF16)
+        w_down[:, part] = dot(inner, rows[1, i], TN).astype(BF16)
+        return carry
+
+    lax.fori_loop(0, CHIPS, grads, 0)
+    stores = [
+        pltpu.make_async_copy(w_gate, gg, local_sems.at[7]),
+        pltpu.make_async_copy(w_up, ug, local_sems.at[8]),
+        pltpu.make_async_copy(w_down, dg, local_sems.at[9]),
+    ]
+    for each in stores:
+        each.start()
+    over(4, hidden_block, lambda i: 4 + i)
+
     def finish(i, carry):
         part = pl.ds(pl.multiple_of(i * 16, 16), 16)
         v = gp_ref[part, :].astype(F32)
         sigma = jax.nn.sigmoid(v)
         grad = hg[part, :]
-        upg_ref[part, :] = (grad * (v * sigma)).astype(BF16)
-        gpg_ref[part, :] = (grad * up_ref[part, :].astype(F32) * slope_of(v, sigma)).astype(BF16)
+        gp_ref[part, :] = (grad * up_ref[part, :].astype(F32) * slope_of(v, sigma)).astype(BF16)
+        up_ref[part, :] = (grad * (v * sigma)).astype(BF16)
         return carry
 
     lax.fori_loop(0, FFD // 16, finish, 0)
+    stores += [
+        pltpu.make_async_copy(gp_ref, gpg, local_sems.at[12]),
+        pltpu.make_async_copy(up_ref, upg, local_sems.at[13]),
+    ]
+    stores[3].start()
+    stores[4].start()
 
     def home_arrival(source):
         return pltpu.make_async_remote_copy(
@@ -549,20 +622,35 @@
     halves = f_recv[...].astype(F32).reshape(WIN, 2, PAD, PAIR)
     combined = (halves[:, 0] + halves[:, 1]).reshape(WIN * PAD, PAIR)
     back[...] = jnp.transpose(combined).astype(BF16)
-    mig_ref[...] = dot(back[lanes, :], picked[...], NN).astype(BF16)
-
-    for o in range(1, 4):
-        z_arrival((z + o) % 4).wait_recv()
-
-    def add_down(i, carry):
-        part = pl.ds(pl.multiple_of(i * 16, 16), 16)
-        total = d_send[r, part].astype(F32)
-        for o in range(1, 4):
-            total = total + z_recv[(z + o) % 4, part].astype(F32)
-        dwg_ref[part, :] = total.astype(BF16)
-        return carry
-
-    lax.fori_loop(0, FFD // 16, add_down, 0)
+    result = li_pair.at[pl.ds(0, FEAT)]
+    result[...] = dot(back[lanes, :], picked[...], NN).astype(BF16)
+    stores.append(pltpu.make_async_copy(result, mig, local_sems.at[14]))
+    stores[5].start()
+
+    wait_z(yl)
+
+    @pl.when(z_mode)
+    def _():
+        y_final.wait_recv()
+
+        def add_both(i, carry):
+            part = pl.ds(pl.multiple_of(i * 16, 16), 16)
+            d_send[r, part] = (sum_z(yl, part, r) + y_last[part, :].astype(F32)).astype(BF16)
+            return carry
+
+        lax.fori_loop(0, FFD // 16, add_both, 0)
+
+    @pl.when(jnp.logical_not(z_mode))
+    def _():
+        def add_z(i, carry):
+            part = pl.ds(pl.multiple_of(i * 16, 16), 16)
+            d_send[r, part] = sum_z(yl, part, r).astype(BF16)
+            return carry
+
+        lax.fori_loop(0, FFD // 16, add_z, 0)
+
+    stores.append(pltpu.make_async_copy(d_send.at[r], dwg, local_sems.at[15]))
+    stores[6].start()
 
     for each in stores:
         each.wait()
@@ -572,14 +660,29 @@
         to_sib(o).wait_send()
         if o:
             to_chip(o).wait_send()
+    @pl.when(k == 1)
+    def _():
+        sib_li.wait_send()
+
     for j in range(8):
-        @pl.when(j // 4 != yl)
+        in_plane = (j % 2 == yh) | ((j // 2 - x) % 2 == 0)
+        to_z = (j % 4 != z) & (in_plane | (j // 4 == yl))
+        to_y = jnp.logical_not(in_plane) & (j // 4 != yl)
+
+        @pl.when(to_z)
         def _(j=j):
-            y_copy(j).wait_send()
-    for to in range(4):
-        @pl.when(to != z)
-        def _(to=to):
-            z_copy(to).wait_send()
+            for p in range(2):
+                z_copy(j, p).wait_send()
+
+        @pl.when(to_y)
+        def _(j=j):
+            for p in range(2):
+                y_copy(j, p).wait_send()
+
+    @pl.when(z_mode)
+    def _():
+        y_final.wait_send()
+
     for i in range(4):
         for core in range(2):
             @pl.when(jnp.logical_not(home_self(i, core)))
@@ -648,15 +751,18 @@
             shape(HID, CHIPS * PAIR), shape(HID, CHIPS * PAIR), shape(HID, CHIPS * PAIR),
             shape(FEAT, TOK),
         ),
-        in_specs=[vmem] * 4 + [hbm] * 6,
-        out_specs=(vmem, vmem, vmem, hbm, hbm, hbm, vmem),
+        in_specs=[vmem] * 2 + [hbm] * 8,
+        out_specs=(hbm,) * 7,
         scratch_shapes=[
+            scratch(FFD, TOK),
+            scratch(FFD, TOK),
             scratch(CHIPS, PAIR, TOK),
             scratch(PAIR, TOK),
             scratch(ROWS, FFD, PAIR),
             scratch(ROWS, FFD, PAIR),
-            scratch(ROWS // 2, FFD, PAIR),
-            scratch(ROWS // 2, FFD, PAIR),
+            scratch(ROWS, FFD, PAIR),
+            scratch(2, FFD, PAIR),
+            scratch(FFD, PAIR),
             scratch(2, CHIPS, SLOTS, PAIR),
             scratch(HID, CHIPS * PAIR),
             scratch(HID, CHIPS * PAIR),

time: 173 us -> 158 us (0.913)
  the two profiles are of different devices: /device:TPU:25 before, /device:TPU:99 now
where the time goes in v3:
time: 158 us
  Pallas kernels  158 us (100%)
    pallas_call x1, Pallas kernels, body(): pl.pallas_call(kernel, out_shape=(shape(FFD, TOK), shape(FFD, TOK), shape...  150 us
    pallas_call x1, Pallas kernels, place(): pl.pallas_call(place_kernel, out_shape=tuple((jax.ShapeDtypeStruct(a.shap...  7.36 us

profile of v3, /device:TPU:99, one launch (start us, length us, event | category | flops | bytes accessed | tf_op | source)
XLA Modules:
  0.0 158.2 jit_solution(2759367240195979036)
XLA Ops:
  0.6 150.2 %layer_backward.1 = (bf16[304,1024]{1,0:T(8,128)(2,1)}, bf16[304,1024]{1,0:T(8,128)(2,1)}, bf16[304,896]{1,0:T(8,128)(2,1)}, bf16[152,7168]{1,0:T(8,128)(2,1)}, ...) custom-call(s32[2,1024]{1,0:T(2,128)} %bitcast.30, f32[2,1024]{1,0:T(2,128)} %bitcast.31, ...), custom_call_target="tpu_custom_call" | custom-call | tf_op jit(solution)/shard_map/layer_backward/pallas_call | solution.py:747
  150.9 7.4 %place_results.1 = (bf16[304,1024]{1,0:T(8,128)(2,1)}, bf16[304,1024]{1,0:T(8,128)(2,1)}, bf16[304,896]{1,0:T(8,128)(2,1)}, bf16[152,7168]{1,0:T(8,128)(2,1)}, b...) custom-call(bf16[304,1024]{1,0:T(8,128)(2,1)} %get-tuple-element.21.refs_0_, ...), custom_call_target="tpu_custom_call" | custom-call | tf_op jit(solution)/shard_map/place_results/pallas_call | solution.py:722

commit v4 on v3

--- a/solution.py
+++ b/solution.py
@@ -363,20 +363,24 @@
 
     across_row = row_of(1 - yl, z)
     z_mode = (z % 2 == yh) | (z // 2 == x % 2)
-    y_final = ch.copy(d_send.at[across_row], y_last, row_dev(across_row))
+    y_final = [
+        ch.copy(d_send.at[across_row, cut], y_last.at[cut], row_dev(across_row)) for cut in cuts
+    ]
 
     def down_cross():
         @pl.when(z_mode)
         def _():
-            wait_z(1 - yl)
-
-            def add_cross(i, carry):
-                part = pl.ds(pl.multiple_of(i * 16, 16), 16)
-                d_send[across_row, part] = sum_z(1 - yl, part, across_row).astype(BF16)
-                return carry
-
-            lax.fori_loop(0, FFD // 16, add_cross, 0)
-            y_final.start()
+            for p in range(2):
+                for o in range(1, 4):
+                    z_arrival(1 - yl, (z + o) % 4, p).wait_recv()
+
+                def add_cross(i, carry, p=p):
+                    part = pl.ds(pl.multiple_of(p * 160 + i * 16, 16), 16)
+                    d_send[across_row, part] = sum_z(1 - yl, part, across_row).astype(BF16)
+                    return carry
+
+                lax.fori_loop(0, 10 - p, add_cross, 0)
+                y_final[p].start()
 
     for each in to_experts:
         each.wait_recv()
@@ -631,7 +635,8 @@
 
     @pl.when(z_mode)
     def _():
-        y_final.wait_recv()
+        for each in y_final:
+            each.wait_recv()
 
         def add_both(i, carry):
             part = pl.ds(pl.multiple_of(i * 16, 16), 16)
@@ -681,7 +686,8 @@
 
     @pl.when(z_mode)
     def _():
-        y_final.wait_send()
+        for each in y_final:
+            each.wait_send()
 
     for i in range(4):
         for core in range(2):

time: 158 us -> 158 us (level)
  no operation moved by 1% of the time
where the time goes in v4:
time: 158 us
  Pallas kernels  158 us (100%)
    pallas_call x1, Pallas kernels, body(): pl.pallas_call(kernel, out_shape=(shape(FFD, TOK), shape(FFD, TOK), shape...  150 us
    pallas_call x1, Pallas kernels, place(): pl.pallas_call(place_kernel, out_shape=tuple((jax.ShapeDtypeStruct(a.shap...  7.36 us

profile of v4, /device:TPU:99, one launch (start us, length us, event | category | flops | bytes accessed | tf_op | source)
XLA Modules:
  0.0 158.2 jit_solution(15925287193157119636)
XLA Ops:
  0.6 150.2 %layer_backward.1 = (bf16[304,1024]{1,0:T(8,128)(2,1)}, bf16[304,1024]{1,0:T(8,128)(2,1)}, bf16[304,896]{1,0:T(8,128)(2,1)}, bf16[152,7168]{1,0:T(8,128)(2,1)}, ...) custom-call(s32[2,1024]{1,0:T(2,128)} %bitcast.30, f32[2,1024]{1,0:T(2,128)} %bitcast.31, ...), custom_call_target="tpu_custom_call" | custom-call | tf_op jit(solution)/shard_map/layer_backward/pallas_call | solution.py:753
  150.9 7.4 %place_results.1 = (bf16[304,1024]{1,0:T(8,128)(2,1)}, bf16[304,1024]{1,0:T(8,128)(2,1)}, bf16[304,896]{1,0:T(8,128)(2,1)}, bf16[152,7168]{1,0:T(8,128)(2,1)}, b...) custom-call(bf16[304,1024]{1,0:T(8,128)(2,1)} %get-tuple-element.21.refs_0_, ...), custom_call_target="tpu_custom_call" | custom-call | tf_op jit(solution)/shard_map/place_results/pallas_call | solution.py:728
